TPU v7x, 512 devices: a whole 4x8x8 slice. The times are simulated.
512 devices in a mesh: img: 32 (over y, z_lo, core), rows: 16 (over z_hi, x).
Axes of the slice: x: 4, y: 8, z: 8 (z_hi: 4, z_lo: 2; z = z_hi * 2 + z_lo), core: 2. Of those that a mesh axis runs over, the one named last changes fastest.
Arguments:
- center_mid: bfloat16 [32, 64, 32, 512], P('img', 'rows'), may hold values from -6 to 6
- radius_mid: bfloat16 [32, 64, 32, 512], P('img', 'rows'), may hold values from 0.049804688 to 1.5
- conv_weight: bfloat16 [512, 3, 3, 512], P('img'), may hold values from -0.09375 to 0.09375
- center_upstream: bfloat16 [32, 64, 32, 512], P('img', 'rows'), may hold values from -6 to 6
- radius_upstream: bfloat16 [32, 64, 32, 512], P('img', 'rows'), may hold values from -6 to 6
Outputs:
- center_mid_grad: bfloat16 [32, 64, 32, 512], P('img', 'rows')
- radius_mid_grad: bfloat16 [32, 64, 32, 512], P('img', 'rows')
- weight_grad: float32 [512, 3, 3, 512], P('img', None, None, 'rows')
All inputs are finite; a program needn't handle non-finite values.
Results may differ from a plain program's by a relative error of at most 0.0055.
Values may be sent and summed in bfloat16 or wider, within the bound.
A program may use at most 64 MiB of HBM per device.

v0:
```python
import jax
import jax.numpy as jnp
from jax import lax
from jax.sharding import PartitionSpec as P


def with_halo(cells, sides, width):
    for axis, dim in sides:
        count = lax.axis_size(axis)
        ends = count - 1
        head = lax.slice_in_dim(cells, 0, width, axis=dim)
        tail = lax.slice_in_dim(cells, cells.shape[dim] - width, cells.shape[dim], axis=dim)
        cells = jnp.concatenate(
            [
                lax.ppermute(tail, axis, [(i, (i + 1) % count) for i in range(ends)]),
                cells,
                lax.ppermute(head, axis, [((i + 1) % count, i) for i in range(ends)]),
            ],
            axis=dim,
        )
    return cells


def pad_columns(block):
    widths = [(0, 0)] * (block.ndim - 2) + [(1, 1), (0, 0)]
    return jnp.pad(block, widths)


def tap_product(left, kernel_tap):
    return lax.dot_general(
        left, kernel_tap, (((left.ndim - 1,), (1,)), ((), ())), preferred_element_type=jnp.float32
    )


def weight_terms(inputs_pad, piece, row_count, col_count):
    terms = []
    for tap_row in range(3):
        for tap_col in range(3):
            window = inputs_pad[
                :, :, tap_row : tap_row + row_count, tap_col : tap_col + col_count, :
            ]
            terms.append(
                lax.dot_general(
                    window,
                    piece,
                    (((1, 2, 3), (1, 2, 3)), ((0,), (0,))),
                    preferred_element_type=jnp.float32,
                )
            )
    stacked = jnp.stack(terms, axis=2)
    return stacked.reshape(stacked.shape[0], stacked.shape[1], 3, 3, stacked.shape[3])


def data_padded(padded, kernel, row_count, col_count):
    total = None
    for tap_row in range(3):
        for tap_col in range(3):
            window = padded[
                :, 2 - tap_row : 2 - tap_row + row_count, 2 - tap_col : 2 - tap_col + col_count, :
            ]
            term = tap_product(window, kernel[:, tap_row, tap_col, :])
            total = term if total is None else total + term
    return total


def layer_back(upstream, weight, inputs_pad):
    row_count = upstream.shape[2]
    col_count = upstream.shape[3]
    batch = inputs_pad.shape[1]
    kernels = (weight, jnp.abs(weight))
    operand = with_halo(upstream, (("rows", 2),), 1)
    padded = pad_columns(lax.all_gather(operand, "img", axis=1, tiled=True))
    inner = padded[:, :, 1 : row_count + 1, 1 : col_count + 1, :]
    running = weight_terms(inputs_pad, inner, row_count, col_count)
    fresh = jnp.stack(
        [data_padded(padded[which], kernels[which], row_count, col_count) for which in range(2)]
    )
    grads = fresh.astype(jnp.bfloat16)
    running, grads = (running, grads)
    image_cot = lax.all_to_all(grads, "img", split_axis=1, concat_axis=4, tiled=True)
    partial_value = (running[0] + jnp.sign(weight.astype(jnp.float32)) * running[1]) / batch
    summed = lax.psum_scatter(partial_value, "rows", scatter_dimension=3, tiled=True)
    return (image_cot, summed)


def on_device(center_mid, radius_mid, conv_weight, center_upstream, radius_upstream):
    stored = jnp.stack([center_mid, radius_mid])
    channel = lax.all_to_all(stored, "img", split_axis=4, concat_axis=1, tiled=True)
    rimmed = with_halo(channel, (("rows", 2),), 1)
    rimmed = pad_columns(rimmed)
    middle = rimmed[0].astype(jnp.float32)
    spread = rimmed[1].astype(jnp.float32)
    act_upper = jnp.maximum(middle + spread, 0.0)
    act_lower = jnp.maximum(middle - spread, 0.0)
    hidden_pad = jnp.stack([(act_upper + act_lower) * 0.5, (act_upper - act_lower) * 0.5]).astype(
        jnp.bfloat16
    )
    upstream = jnp.stack([center_upstream, radius_upstream])
    hidden_cot, weight_grad = layer_back(upstream, conv_weight, hidden_pad)
    upper_on = (center_mid > -radius_mid).astype(jnp.float32)
    lower_on = (center_mid > radius_mid).astype(jnp.float32)
    center_part = hidden_cot[0].astype(jnp.float32)
    radius_part = hidden_cot[1].astype(jnp.float32)
    upper_cot = 0.5 * (center_part + radius_part) * upper_on
    lower_cot = 0.5 * (center_part - radius_part) * lower_on
    center_mid_grad = (upper_cot + lower_cot).astype(jnp.bfloat16)
    radius_mid_grad = (upper_cot - lower_cot).astype(jnp.bfloat16)
    return (center_mid_grad, radius_mid_grad, weight_grad)


def solution(mesh):
    placed = (
        P("img", "rows", None, None),
        P("img", "rows", None, None),
        P("img", None, None, None),
        P("img", "rows", None, None),
        P("img", "rows", None, None),
    )
    return jax.shard_map(
        on_device,
        mesh=mesh,
        in_specs=placed,
        out_specs=(
            P("img", "rows", None, None),
            P("img", "rows", None, None),
            P("img", None, None, "rows"),
        ),
        check_vma=False,
    )
```

profile of v0, /device:TPU:8, one launch (start us, length us, event | category | flops | bytes accessed | tf_op | source)
XLA Modules:
  0.0 319.0 jit_solution(3447518856735842004)
XLA Ops:
  7.2 0.9 pad_maximum_fusion.6
  8.2 3.4 %collective-permute-start = (bf16[2,1,1,32,512]{4,3,2,1,0:T(8,128)(2,1)S(1)}, bf16[2,1,1,32,512]{4,3,2,1,0:T(8,128)(2,1)S(1)}, u32[]{:S(2)}, u32[]{:S(2)}) collective-permute-start(bf16[2,1,1,32,512]{4,3,2,1,0:T(8,128)(2,1)S(1)} %get-tuple-element.21), channel_id=1, source_target_pairs={{0,1},{1,2},{2,3},{3,4},{4,5},{5,6},{6,7},{7,8},{8,9},{9,10},{10,1... | collective-permute-start | bytes 196616 | tf_op jit(solution)/shard_map/ppermute | solution.py:15
  11.6 1.3 collective-permute-start.1
  12.9 0.6 collective-permute-done
  13.5 4.3 %collective-permute-done.1 = bf16[2,1,1,32,512]{4,3,2,1,0:T(8,128)(2,1)S(1)} collective-permute-done((bf16[2,1,1,32,512]{4,3,2,1,0:T(8,128)(2,1)S(1)}, bf16[2,1,1,32,512]{4,3,2,1,0:T(8,128)(2,1)S(1)}, u32[]{:S(2)}, u32[]{:S(2)}) %collective-permute-start.1) | collective-permute-done | bytes 65568 | tf_op jit(solution)/shard_map/ppermute | solution.py:17
  17.7 1.8 pad_maximum_fusion.3
  19.5 1.0 pad_maximum_fusion.4
  20.5 0.7 copy.26
  21.2 1.0 reshape.102
  22.3 20.8 %all_to_all.33 = bf16[32,2,2048]{2,1,0:T(2,128)(2,1)S(1)} all-to-all(bf16[32,2,2048]{2,1,0:T(2,128)(2,1)S(1)} %reshape.102), channel_id=1, replica_groups=mesh['img'=32,'rows'=16] {'img'}, dimensions={0} | all-to-all | bytes 524288 | tf_op jit(solution)/shard_map/all_to_all | solution.py:88
  43.1 0.5 reshape.103
  43.6 0.3 copy.91
  43.9 3.4 %collective-permute-start.2 = (bf16[2,32,1,32,16]{3,4,2,0,1:T(8,128)(2,1)S(1)}, bf16[2,32,1,32,16]{3,4,2,0,1:T(8,128)(2,1)S(1)}, u32[]{:S(2)}, u32[]{:S(2)}) collective-permute-start(bf16[2,32,1,32,16]{3,4,2,0,1:T(8,128)(2,1)S(1)} %get-tuple-element.15), channel_id=1, source_target_pairs={{0,1},{1,2},{2,3},{3,4},{4,5},{5,6},{6,7},{7,8},{8,9},{9,10},{10,1... | collective-permute-start | bytes 196616 | tf_op jit(solution)/shard_map/ppermute | solution.py:15
  47.3 1.3 collective-permute-start.3
  48.7 1.0 copy.19
  49.7 1.1 copy.20
  50.8 1.8 collective-permute-done.2
  52.6 5.7 %collective-permute-done.3 = bf16[2,32,1,32,16]{3,4,2,0,1:T(8,128)(2,1)S(1)} collective-permute-done((bf16[2,32,1,32,16]{3,4,2,0,1:T(8,128)(2,1)S(1)}, bf16[2,32,1,32,16]{3,4,2,0,1:T(8,128)(2,1)S(1)}, u32[]{:S(2)}, u32[]{:S(2)}) %collective-permute-start.3) | collective-permute-done | bytes 65568 | tf_op jit(solution)/shard_map/ppermute | solution.py:17
  58.2 0.8 fusion.43
  59.1 0.6 multiply_convert_fusion
  59.7 55.6 %all-gather.2.cloned.1.call-done = bf16[2,32,6,32,512]{4,3,2,1,0:T(8,128)(2,1)} async-done(((bf16[2,1,6,32,512]{4,3,2,1,0:T(8,128)(2,1)}), bf16[2,32,6,32,512]{4,3,2,1,0:T(8,128)(2,1)}) %all-gather.2.cloned.1.call-update) | async-done | bytes 12582928 | tf_op jit(solution)/shard_map/all_gather | solution.py:72
  115.3 10.8 %fusion = (bf16[32,6,34,512]{3,2,1,0:T(8,128)(2,1)S(1)}, bf16[32,6,34,512]{3,2,1,0:T(8,128)(2,1)S(1)}) fusion(bf16[2,32,6,32,512]{4,3,2,1,0:T(8,128)(2,1)} %all-gather.2.cloned.1.call-done), kind=kLoop, calls=%fused_computation.2 | loop fusion | bytes 25952256 | tf_op jit(solution)/shard_map/squeeze | solution.py:76
  126.1 2.8 fusion.34
  128.9 2.8 fusion.28
  131.8 2.8 fusion.30
  134.6 2.8 fusion.22
  137.5 2.8 fusion.24
  140.3 3.1 fusion.16
  143.4 2.8 fusion.10
  146.2 2.8 fusion.12
  149.1 2.8 fusion.4
  151.9 2.8 fusion.6
  154.7 2.9 fusion.88
  157.6 3.3 %fusion.85 = f32[32,4,32,16]{2,3,1,0:T(8,128)S(1)} fusion(f32[32,4,32,16]{2,3,1,0:T(8,128)S(1)} %fusion.28, f32[32,4,32,16]{2,3,1,0:T(8,128)S(1)} %fusion.30, f32[32,4,32,16]{2,3,1,0:T(8,128)S(1)} %fusion.88, bf16[32,6,34,512]{3,2,1,0:T(8,128)(2,1)S(1)} %get-tuple-element.9, bf16[16,3,3,512]{3,0,2,1:T(8,128)(2,1)S(1)} %copy-done.2), kind=kOutput, calls=%fused_computation.83 | convolution fusion | flops 67305472 | bytes 7618560 | tf_op jit(solution)/shard_map/dot_general | solution.py:30
  160.9 2.9 fusion.79
  163.8 2.8 fusion.100
  166.6 2.8 fusion.91
  169.5 2.9 fusion.73
  172.4 2.9 fusion.67
  175.3 2.9 fusion.103
  178.1 0.3 copy_bitcast_fusion.1
  178.4 1.7 reshape.100
  180.2 5.5 %all-to-all-start = ((bf16[32,2,2048]{2,1,0:T(2,128)(2,1)}), bf16[32,2,2048]{2,1,0:T(2,128)(2,1)}, u32[]{:S(2)}, u32[]{:S(2)}) async-start(bf16[32,2,2048]{2,1,0:T(2,128)(2,1)} %reshape.100), calls=%async_computation | async-start | bytes 524288 | tf_op jit(solution)/shard_map/all_to_all | solution.py:80
  185.7 4.6 %fusion.114 = f32[2,16,9,512]{3,1,0,2:T(8,128)S(1)} fusion(bf16[1,32,6,34,16]{3,4,2,0,1:T(8,128)(2,1)S(1)} %get-tuple-element.14, bf16[1,32,6,34,16]{3,4,2,0,1:T(8,128)(2,1)S(1)} %get-tuple-element.13, bf16[2,32,6,32,512]{4,3,2,1,0:T(8,128)(2,1)} %all-gather.2.cloned.1.call-done), kind=kOutput, calls=%fused_computation.109 | convolution fusion | flops 134348800 | bytes 8871936 | tf_op jit(solution)/shard_map/dot_general | solution.py:43
  190.3 4.9 %fusion.113 = f32[2,16,9,512]{3,1,0,2:T(8,128)S(1)} fusion(f32[2,16,9,512]{3,1,0,2:T(8,128)S(1)} %fusion.114, bf16[1,32,6,34,16]{3,4,2,0,1:T(8,128)(2,1)S(1)} %get-tuple-element.14, bf16[1,32,6,34,16]{3,4,2,0,1:T(8,128)(2,1)S(1)} %get-tuple-element.13, bf16[2,32,6,32,512]{4,3,2,1,0:T(8,128)(2,1)} %all-gather.2.cloned.1.call-done), kind=kOutput, calls=%fused_computation.107 | convolution fusion | flops 134348800 | bytes 10027008 | tf_op jit(solution)/shard_map/dot_general | solution.py:43
  195.2 0.3 slice-done.2
  195.5 1.9 fusion.112
  197.4 1.4 fusion.111
  198.8 1.9 fusion.110
  200.7 1.9 fusion.109
  202.6 1.5 fusion.108
  204.1 1.9 fusion.107
  206.0 1.9 fusion.106
  208.0 1.5 copy.69
  209.5 2.1 reshape.98
  211.7 2.0 reshape.101
  213.7 0.3 bitcast_bitcast_fusion
  214.0 0.3 fusion.115
  214.5 0.4 subtract_convert_fusion
  214.9 0.8 copy.38
  215.8 0.8 copy.39
  216.6 93.7 %reduce-scatter.4.cloned.1.call-done = f32[32,144]{1,0:T(8,128)} async-done(((f32[512,144]{1,0:T(8,128)}), f32[32,144]{1,0:T(8,128)}) %reduce-scatter.4.cloned.1.call-update) | async-done | bytes 18448
  310.4 0.9 reshape.99
  311.3 0.8 copy.70
  (27 shorter events, 0.5 us)
Async XLA Ops:
  7.2 42.5 %copy-start.4 = (bf16[1,4,32,512]{3,2,1,0:T(8,128)(2,1)S(1)}, bf16[1,4,32,512]{3,2,1,0:T(8,128)(2,1)}, u32[]{:S(2)}) copy-start(bf16[1,4,32,512]{3,2,1,0:T(8,128)(2,1)} %param.5) | copy-start | bytes 393220
  7.2 41.5 %copy-start.3 = (bf16[1,4,32,512]{3,2,1,0:T(8,128)(2,1)S(1)}, bf16[1,4,32,512]{3,2,1,0:T(8,128)(2,1)}, u32[]{:S(2)}) copy-start(bf16[1,4,32,512]{3,2,1,0:T(8,128)(2,1)} %param.6) | copy-start | bytes 393220
  7.2 43.5 %copy-start.2 = (bf16[16,3,3,512]{3,0,2,1:T(8,128)(2,1)S(1)}, bf16[16,3,3,512]{3,0,2,1:T(8,128)(2,1)}, u32[]{:S(2)}) copy-start(bf16[16,3,3,512]{3,0,2,1:T(8,128)(2,1)} %param.7) | copy-start | bytes 442372
  7.2 108.1 %all-gather.2.cloned.1.call-start = ((), (), s32[]{:S(2)}) async-start(), calls=%async_computation.3 | async-start | bytes 12976128 | tf_op jit(solution)/shard_map/all_gather | solution.py:72
  8.2 5.3 %collective-permute-start = (bf16[2,1,1,32,512]{4,3,2,1,0:T(8,128)(2,1)S(1)}, bf16[2,1,1,32,512]{4,3,2,1,0:T(8,128)(2,1)S(1)}, u32[]{:S(2)}, u32[]{:S(2)}) collective-permute-start(bf16[2,1,1,32,512]{4,3,2,1,0:T(8,128)(2,1)S(1)} %get-tuple-element.21), channel_id=1, source_target_pairs={{0,1},{1,2},{2,3},{3,4},{4,5},{5,6},{6,7},{7,8},{8,9},{9,10},{10,1... | collective-permute-start | bytes 196616 | tf_op jit(solution)/shard_map/ppermute | solution.py:15
  11.6 6.2 %collective-permute-start.1 = (bf16[2,1,1,32,512]{4,3,2,1,0:T(8,128)(2,1)S(1)}, bf16[2,1,1,32,512]{4,3,2,1,0:T(8,128)(2,1)S(1)}, u32[]{:S(2)}, u32[]{:S(2)}) collective-permute-start(bf16[2,1,1,32,512]{4,3,2,1,0:T(8,128)(2,1)S(1)} %get-tuple-element.22), channel_id=1, source_target_pairs={{1,0},{2,1},{3,2},{4,3},{5,4},{6,5},{7,6},{8,7},{9,8},{10,9},{11,1... | collective-permute-start | bytes 196616 | tf_op jit(solution)/shard_map/ppermute | solution.py:17
  43.9 8.7 %collective-permute-start.2 = (bf16[2,32,1,32,16]{3,4,2,0,1:T(8,128)(2,1)S(1)}, bf16[2,32,1,32,16]{3,4,2,0,1:T(8,128)(2,1)S(1)}, u32[]{:S(2)}, u32[]{:S(2)}) collective-permute-start(bf16[2,32,1,32,16]{3,4,2,0,1:T(8,128)(2,1)S(1)} %get-tuple-element.15), channel_id=1, source_target_pairs={{0,1},{1,2},{2,3},{3,4},{4,5},{5,6},{6,7},{7,8},{8,9},{9,10},{10,1... | collective-permute-start | bytes 196616 | tf_op jit(solution)/shard_map/ppermute | solution.py:15
  47.3 10.9 %collective-permute-start.3 = (bf16[2,32,1,32,16]{3,4,2,0,1:T(8,128)(2,1)S(1)}, bf16[2,32,1,32,16]{3,4,2,0,1:T(8,128)(2,1)S(1)}, u32[]{:S(2)}, u32[]{:S(2)}) collective-permute-start(bf16[2,32,1,32,16]{3,4,2,0,1:T(8,128)(2,1)S(1)} %get-tuple-element.16), channel_id=1, source_target_pairs={{1,0},{2,1},{3,2},{4,3},{5,4},{6,5},{7,6},{8,7},{9,8},{10,9},{11,1... | collective-permute-start | bytes 196616 | tf_op jit(solution)/shard_map/ppermute | solution.py:17
  180.2 31.5 %all-to-all-start = ((bf16[32,2,2048]{2,1,0:T(2,128)(2,1)}), bf16[32,2,2048]{2,1,0:T(2,128)(2,1)}, u32[]{:S(2)}, u32[]{:S(2)}) async-start(bf16[32,2,2048]{2,1,0:T(2,128)(2,1)} %reshape.100), calls=%async_computation | async-start | bytes 524288 | tf_op jit(solution)/shard_map/all_to_all | solution.py:80
  185.7 124.7 %reduce-scatter.4.cloned.1.call-start = ((), (), s32[]{:S(2)}) async-start(), calls=%async_computation.4 | async-start | bytes 557056
  185.7 9.5 %slice-start = ((s8[12582912]{0:T(1024)(128)(4,1)}), s8[4194304]{0:T(1024)(128)(4,1)S(1)}, s32[]{:S(2)}) async-start(s8[12582912]{0:T(1024)(128)(4,1)} %bitcast.233), calls=%async_computation.5 | async-start | bytes 8388608
  185.7 9.5 %slice-start.1 = ((s8[12582912]{0:T(1024)(128)(4,1)}), s8[4194304]{0:T(1024)(128)(4,1)S(1)}, s32[]{:S(2)}) async-start(s8[12582912]{0:T(1024)(128)(4,1)} %bitcast.233), calls=%async_computation.6 | async-start | bytes 8388608
  190.3 5.2 %slice-start.2 = ((s8[12582912]{0:T(1024)(128)(4,1)}), s8[4194304]{0:T(1024)(128)(4,1)S(1)}, s32[]{:S(2)}) async-start(s8[12582912]{0:T(1024)(128)(4,1)} %bitcast.233), calls=%async_computation.7 | async-start | bytes 8388608
  211.6 2.9 copy-start
  211.6 2.9 copy-start.1
Sparse Core Ops, SparseCore 0:
  19.7 95.5 all-gather.1
  211.8 98.5 reduce-scatter.3
where the time goes:
time: 325 us; the launch traced here: 319 us
  waiting for transfers between devices  162 us (50%)
  matrix products  73.8 us (23%)
  local copies, waits for them, and re-layouts  26.9 us (8%)
  blocking collectives  20.8 us (6%)
  starting transfers between devices  15 us (5%)
  between operations  14.5 us (4%)
  other arithmetic  6.35 us (2%)
    unnamed x3, waiting for transfers between devices  93.8 us
    all_gather x1, waiting for transfers between devices, layer_back(): padded = pad_columns(lax.all_gather(operand, 'img', axis=1, tiled=True))  55.6 us
    dot_general x18, matrix products, tap_product(): lax.dot_general(left, kernel_tap, (((left.ndim - 1,), (1,)), ((), ())), p...  52 us
    dot_general x9, matrix products, weight_terms(): lax.dot_general(window, piece, (((1, 2, 3), (1, 2, 3)), ((0,), (0,))), pr...  21.8 us
    all_to_all x1, blocking collectives, on_device(): lax.all_to_all(stored, 'img', split_axis=4, concat_axis=1, tiled=True)  20.8 us
    unnamed x28, local copies, waits for them, and re-layouts  14.6 us
    squeeze x1, local copies, waits for them, and re-layouts, layer_back(): padded[which]  10.8 us
    ppermute x2, waiting for transfers between devices, with_halo(): lax.ppermute(head, axis, [((i + 1) % count, i) for i in range(ends)])  9.94 us
  transfers between devices with their start and end apart: 7, of which 6 were waited for; matrix products, arithmetic and copies ran while one was open for 12% of the time, Pallas kernels for 0%

commit v1 on v0

--- a/solution.py
+++ b/solution.py
@@ -2,6 +2,11 @@
 import jax.numpy as jnp
 from jax import lax
 from jax.sharding import PartitionSpec as P
+
+
+def all_by_exchange(x, name, dim):
+    sent = jnp.stack([x] * lax.axis_size(name))
+    return jnp.concatenate(lax.all_to_all(sent, name, 0, 0), axis=dim)
 
 
 def with_halo(cells, sides, width):
@@ -69,7 +74,7 @@
     batch = inputs_pad.shape[1]
     kernels = (weight, jnp.abs(weight))
     operand = with_halo(upstream, (("rows", 2),), 1)
-    padded = pad_columns(lax.all_gather(operand, "img", axis=1, tiled=True))
+    padded = pad_columns(all_by_exchange(operand, "img", 1))
     inner = padded[:, :, 1 : row_count + 1, 1 : col_count + 1, :]
     running = weight_terms(inputs_pad, inner, row_count, col_count)
     fresh = jnp.stack(

time: 325 us -> 560 us (1.72)
  waiting for transfers between devices: 162 us -> 366 us
  blocking collectives: 20.8 us -> 0 us
  matrix products: 73.8 us -> 92.8 us
  starting transfers between devices: 15 us -> 32.8 us
  local copies, waits for them, and re-layouts: 26.9 us -> 39.9 us
    all_to_all x0 -> x2, waiting for transfers between devices: none -> 257 us  [the longest x1 257 us: all_by_exchange(): return jnp.concatenate(lax.all_to_all(sent, name, 0, 0), axis=dim)]
    all_gather x1 -> x0, waiting for transfers between devices: 55.6 us -> none  [layer_back(): padded = pad_columns(lax.all_gather(operand, 'img', axis=1, tiled=True))]
    all_to_all x1 -> x0, blocking collectives: 20.8 us -> none  [on_device(): lax.all_to_all(stored, 'img', split_axis=4, concat_axis=1, tiled=True)]
    all_to_all x0 -> x2, starting transfers between devices: none -> 17.9 us  [the longest x1 9.51 us: on_device(): lax.all_to_all(stored, 'img', split_axis=4, concat_axis=1, tiled=True)]
    dot_general x9, matrix products: 21.8 us -> 34.3 us  [weight_terms(): lax.dot_general(window, piece, (((1, 2, 3), (1, 2, 3)), ((0,), (0,))), pr...]
    dot_general x18, matrix products: 52 us -> 58.5 us  [tap_product(): lax.dot_general(left, kernel_tap, (((left.ndim - 1,), (1,)), ((), ())), p...]
    all_to_all x0 -> x1, local copies, waits for them, and re-layouts: none -> 6.23 us  [all_by_exchange(): return jnp.concatenate(lax.all_to_all(sent, name, 0, 0), axis=dim)]
    another operation x0 -> x1, local copies, waits for them, and re-layouts: none -> 6.14 us  [all_by_exchange(): sent = jnp.stack([x] * lax.axis_size(name))]
  transfers between devices with their start and end apart: 7 -> 8, of which waited for: 6 -> 8; matrix products, arithmetic and copies ran while one was open for 12% -> 4% of each run, Pallas kernels for 0% -> 0%
where the time goes in v1:
time: 560 us; the launch traced here: 552 us
  waiting for transfers between devices  366 us (65%)
  matrix products  92.8 us (17%)
  local copies, waits for them, and re-layouts  39.9 us (7%)
  starting transfers between devices  32.8 us (6%)
  between operations  14.6 us (3%)
  other arithmetic  6.71 us (1%)
    all_to_all x1, waiting for transfers between devices, all_by_exchange(): return jnp.concatenate(lax.all_to_all(sent, name, 0, 0), axis=dim)  257 us
    unnamed x2, waiting for transfers between devices  94.5 us
    dot_general x18, matrix products, tap_product(): lax.dot_general(left, kernel_tap, (((left.ndim - 1,), (1,)), ((), ())), p...  58.5 us
    dot_general x9, matrix products, weight_terms(): lax.dot_general(window, piece, (((1, 2, 3), (1, 2, 3)), ((0,), (0,))), pr...  34.3 us
    unnamed x34, local copies, waits for them, and re-layouts  14.9 us
  transfers between devices with their start and end apart: 8, of which 8 were waited for; matrix products, arithmetic and copies ran while one was open for 4% of the time, Pallas kernels for 0%

profile of v1, /device:TPU:8, one launch (start us, length us, event | category | flops | bytes accessed | tf_op | source)
XLA Modules:
  0.0 552.4 jit_solution(7578085973933265606)
XLA Ops:
  7.2 1.0 pad_maximum_fusion.3
  8.2 0.7 copy.27
  8.9 1.7 reshape.113
  10.6 9.5 %all-to-all-start.2 = ((bf16[32,2,2048]{2,1,0:T(2,128)(2,1)}), bf16[32,2,2048]{2,1,0:T(2,128)(2,1)S(1)}, u32[]{:S(2)}, u32[]{:S(2)}) async-start(bf16[32,2,2048]{2,1,0:T(2,128)(2,1)} %reshape.113), calls=%async_computation.2 | async-start | bytes 524288 | tf_op jit(solution)/shard_map/all_to_all | solution.py:93
  20.1 0.8 pad_maximum_fusion.5
  20.9 3.4 collective-permute-start
  24.3 1.3 collective-permute-start.1
  25.6 0.6 collective-permute-done
  26.2 4.3 collective-permute-done.1
  30.5 1.0 maximum_bitcast_fusion
  31.6 6.1 %stack.49 = bf16[32,2,1,6,32,512]{5,4,3,1,2,0:T(8,128)(2,1)} broadcast(bf16[2,6,32,512]{3,2,1,0:T(8,128)(2,1)S(1)} %maximum_bitcast_fusion), dimensions={1,3,4,5} | broadcast | bytes 12976128 | tf_op jit(solution)/shard_map/stack | solution.py:8
  37.8 8.4 %all-to-all-start = ((bf16[32,2,1,6,32,512]{5,4,3,1,2,0:T(8,128)(2,1)}), bf16[32,2,1,6,32,512]{5,4,3,1,2,0:T(8,128)(2,1)}, u32[]{:S(2)}, u32[]{:S(2)}) async-start(bf16[32,2,1,6,32,512]{5,4,3,1,2,0:T(8,128)(2,1)} %stack.49), calls=%async_computation | async-start | bytes 25165824 | tf_op jit(solution)/shard_map/all_to_all | solution.py:9
  46.2 0.5 reshape.114
  47.0 3.4 collective-permute-start.2
  50.4 1.3 collective-permute-start.3
  51.7 1.0 copy.19
  52.8 1.0 copy.20
  53.8 2.4 collective-permute-done.2
  56.3 5.7 %collective-permute-done.3 = bf16[2,32,1,32,16]{3,4,2,0,1:T(8,128)(2,1)S(1)} collective-permute-done((bf16[2,32,1,32,16]{3,4,2,0,1:T(8,128)(2,1)S(1)}, bf16[2,32,1,32,16]{3,4,2,0,1:T(8,128)(2,1)S(1)}, u32[]{:S(2)}, u32[]{:S(2)}) %collective-permute-start.3) | collective-permute-done | bytes 65568 | tf_op jit(solution)/shard_map/ppermute | solution.py:22
  61.9 0.8 fusion.43
  62.8 1.8 multiply_convert_fusion
  64.6 256.8 %all-to-all-done = bf16[32,2,1,6,32,512]{5,4,3,1,2,0:T(8,128)(2,1)} async-done(((bf16[32,2,1,6,32,512]{5,4,3,1,2,0:T(8,128)(2,1)}), bf16[32,2,1,6,32,512]{5,4,3,1,2,0:T(8,128)(2,1)}, u32[]{:S(2)}, u32[]{:S(2)}) %all-to-all-start) | async-done | bytes 12582944 | tf_op jit(solution)/shard_map/all_to_all | solution.py:9
  321.4 6.2 %copy.93 = bf16[32,2,1,6,32,512]{5,4,3,0,1,2:T(8,128)(2,1)S(1)} copy(bf16[32,2,1,6,32,512]{5,4,3,1,2,0:T(8,128)(2,1)} %all-to-all-done) | data formatting | bytes 25165824 | tf_op jit(solution)/shard_map/all_to_all | solution.py:9
  327.7 10.1 %fusion = (bf16[32,6,34,512]{3,2,1,0:T(8,128)(2,1)S(1)}, bf16[32,6,34,512]{3,2,1,0:T(8,128)(2,1)S(1)}) fusion(bf16[2,32,6,32,512]{4,3,2,1,0:T(8,128)(2,1)S(1)} %bitcast.240), kind=kLoop, calls=%fused_computation.3 | loop fusion | bytes 25952256 | tf_op jit(solution)/shard_map/squeeze | solution.py:81
  337.8 3.8 fusion.34
  341.6 2.8 fusion.28
  344.4 2.8 fusion.30
  347.3 2.8 fusion.22
  350.1 2.8 fusion.24
  353.0 4.1 fusion.16
  357.1 2.8 fusion.10
  359.9 2.8 fusion.12
  362.7 2.8 fusion.4
  365.6 3.6 fusion.6
  369.1 3.3 fusion.114
  372.5 3.7 fusion.113
  376.2 4.1 fusion.112
  380.3 3.3 fusion.111
  383.6 3.7 fusion.110
  387.3 3.7 fusion.109
  391.0 3.3 fusion.108
  394.3 3.7 fusion.107
  398.0 4.0 fusion.88
  402.1 2.9 fusion.85
  405.0 2.9 fusion.79
  407.8 3.0 fusion.100
  410.8 3.6 fusion.91
  414.4 3.6 fusion.73
  418.0 3.6 fusion.67
  421.6 3.7 fusion.103
  425.6 1.7 reshape.111
  427.3 5.5 all-to-all-start.1
  432.9 5.4 fusion.106
  438.3 1.1 fusion.171
  439.5 1.5 copy.70
  441.0 2.1 reshape.109
  443.1 1.2 all-to-all-done.1
  444.3 1.9 reshape.112
  447.1 0.4 subtract_convert_fusion
  447.5 0.8 copy.39
  448.3 0.8 copy.40
  449.2 94.5 %reduce-scatter.4.cloned.1.call-done = f32[32,144]{1,0:T(8,128)} async-done(((f32[512,144]{1,0:T(8,128)}), f32[32,144]{1,0:T(8,128)}) %reduce-scatter.4.cloned.1.call-update) | async-done | bytes 18448
  543.7 0.9 reshape.110
  544.6 0.8 copy.71
  (34 shorter events, 1.7 us)
Async XLA Ops:
  10.6 21.0 %all-to-all-start.2 = ((bf16[32,2,2048]{2,1,0:T(2,128)(2,1)}), bf16[32,2,2048]{2,1,0:T(2,128)(2,1)S(1)}, u32[]{:S(2)}, u32[]{:S(2)}) async-start(bf16[32,2,2048]{2,1,0:T(2,128)(2,1)} %reshape.113), calls=%async_computation.2 | async-start | bytes 524288 | tf_op jit(solution)/shard_map/all_to_all | solution.py:93
  20.9 5.3 collective-permute-start
  24.3 6.2 %collective-permute-start.1 = (bf16[2,1,1,32,512]{4,3,2,1,0:T(8,128)(2,1)S(1)}, bf16[2,1,1,32,512]{4,3,2,1,0:T(8,128)(2,1)S(1)}, u32[]{:S(2)}, u32[]{:S(2)}) collective-permute-start(bf16[2,1,1,32,512]{4,3,2,1,0:T(8,128)(2,1)S(1)} %get-tuple-element.22), channel_id=1, source_target_pairs={{1,0},{2,1},{3,2},{4,3},{5,4},{6,5},{7,6},{8,7},{9,8},{10,9},{11,1... | collective-permute-start | bytes 196616 | tf_op jit(solution)/shard_map/ppermute | solution.py:22
  37.8 14.0 %copy-start.7 = (bf16[1,4,32,512]{3,2,1,0:T(8,128)(2,1)S(1)}, bf16[1,4,32,512]{3,2,1,0:T(8,128)(2,1)}, u32[]{:S(2)}) copy-start(bf16[1,4,32,512]{3,2,1,0:T(8,128)(2,1)} %param.6) | copy-start | bytes 393220
  37.8 15.0 %copy-start.8 = (bf16[1,4,32,512]{3,2,1,0:T(8,128)(2,1)S(1)}, bf16[1,4,32,512]{3,2,1,0:T(8,128)(2,1)}, u32[]{:S(2)}) copy-start(bf16[1,4,32,512]{3,2,1,0:T(8,128)(2,1)} %param.5) | copy-start | bytes 393220
  37.8 16.0 %copy-start.5 = (bf16[16,3,3,512]{3,0,2,1:T(8,128)(2,1)S(1)}, bf16[16,3,3,512]{3,0,2,1:T(8,128)(2,1)}, u32[]{:S(2)}) copy-start(bf16[16,3,3,512]{3,0,2,1:T(8,128)(2,1)} %param.7) | copy-start | bytes 442372
  37.8 283.7 %all-to-all-start = ((bf16[32,2,1,6,32,512]{5,4,3,1,2,0:T(8,128)(2,1)}), bf16[32,2,1,6,32,512]{5,4,3,1,2,0:T(8,128)(2,1)}, u32[]{:S(2)}, u32[]{:S(2)}) async-start(bf16[32,2,1,6,32,512]{5,4,3,1,2,0:T(8,128)(2,1)} %stack.49), calls=%async_computation | async-start | bytes 25165824 | tf_op jit(solution)/shard_map/all_to_all | solution.py:9
  47.0 9.3 %collective-permute-start.2 = (bf16[2,32,1,32,16]{3,4,2,0,1:T(8,128)(2,1)S(1)}, bf16[2,32,1,32,16]{3,4,2,0,1:T(8,128)(2,1)S(1)}, u32[]{:S(2)}, u32[]{:S(2)}) collective-permute-start(bf16[2,32,1,32,16]{3,4,2,0,1:T(8,128)(2,1)S(1)} %get-tuple-element.15), channel_id=1, source_target_pairs={{0,1},{1,2},{2,3},{3,4},{4,5},{5,6},{6,7},{7,8},{8,9},{9,10},{10,1... | collective-permute-start | bytes 196616 | tf_op jit(solution)/shard_map/ppermute | solution.py:20
  50.4 11.5 %collective-permute-start.3 = (bf16[2,32,1,32,16]{3,4,2,0,1:T(8,128)(2,1)S(1)}, bf16[2,32,1,32,16]{3,4,2,0,1:T(8,128)(2,1)S(1)}, u32[]{:S(2)}, u32[]{:S(2)}) collective-permute-start(bf16[2,32,1,32,16]{3,4,2,0,1:T(8,128)(2,1)S(1)} %get-tuple-element.16), channel_id=1, source_target_pairs={{1,0},{2,1},{3,2},{4,3},{5,4},{6,5},{7,6},{8,7},{9,8},{10,9},{11,1... | collective-permute-start | bytes 196616 | tf_op jit(solution)/shard_map/ppermute | solution.py:22
  53.8 308.9 %copy-start.9 = (bf16[16,3,3,512]{3,0,2,1:T(8,128)(2,1)}, bf16[16,3,3,512]{3,0,2,1:T(8,128)(2,1)S(1)}, u32[]{:S(2)}) copy-start(bf16[16,3,3,512]{3,0,2,1:T(8,128)(2,1)S(1)} %abs.3) | copy-start | bytes 442372
  327.7 66.6 %copy-start = (bf16[32,2,1,6,32,512]{5,4,3,0,1,2:T(8,128)(2,1)}, bf16[32,2,1,6,32,512]{5,4,3,0,1,2:T(8,128)(2,1)S(1)}, u32[]{:S(2)}) copy-start(bf16[32,2,1,6,32,512]{5,4,3,0,1,2:T(8,128)(2,1)S(1)} %copy.93) | copy-start | bytes 37748740
  405.0 5.9 %copy-start.10 = (f32[32,4,32,16]{2,3,1,0:T(8,128)S(1)}, f32[32,4,32,16]{2,3,1,0:T(8,128)}, u32[]{:S(2)}) copy-start(f32[32,4,32,16]{2,3,1,0:T(8,128)} %fusion.16) | copy-start | bytes 786436
  421.6 11.3 %copy-start.3 = (bf16[1,32,6,34,16]{3,4,2,0,1:T(8,128)(2,1)S(1)}, bf16[1,32,6,34,16]{3,4,2,0,1:T(8,128)(2,1)}, u32[]{:S(2)}) copy-start(bf16[1,32,6,34,16]{3,4,2,0,1:T(8,128)(2,1)} %get-tuple-element.13) | copy-start | bytes 626692
  421.6 11.3 %copy-start.4 = (bf16[1,32,6,34,16]{3,4,2,0,1:T(8,128)(2,1)S(1)}, bf16[1,32,6,34,16]{3,4,2,0,1:T(8,128)(2,1)}, u32[]{:S(2)}) copy-start(bf16[1,32,6,34,16]{3,4,2,0,1:T(8,128)(2,1)} %get-tuple-element.14) | copy-start | bytes 626692
  427.3 17.0 %all-to-all-start.1 = ((bf16[32,2,2048]{2,1,0:T(2,128)(2,1)}), bf16[32,2,2048]{2,1,0:T(2,128)(2,1)}, u32[]{:S(2)}, u32[]{:S(2)}) async-start(bf16[32,2,2048]{2,1,0:T(2,128)(2,1)} %reshape.111), calls=%async_computation.1 | async-start | bytes 524288 | tf_op jit(solution)/shard_map/all_to_all | solution.py:85
  432.8 6.6 %copy-start.6 = (bf16[16,3,3,512]{3,0,2,1:T(8,128)(2,1)S(1)}, bf16[16,3,3,512]{3,0,2,1:T(8,128)(2,1)}, u32[]{:S(2)}) copy-start(bf16[16,3,3,512]{3,0,2,1:T(8,128)(2,1)} %param.7) | copy-start | bytes 442372
  432.8 110.9 %reduce-scatter.4.cloned.1.call-start = ((), (), s32[]{:S(2)}) async-start(), calls=%async_computation.4 | async-start | bytes 557056
  443.1 4.0 copy-start.1
  443.1 4.0 copy-start.2
Sparse Core Ops, SparseCore 0:
  443.2 100.3 reduce-scatter.3
